TPU v7x, 32 devices: a whole 2x2x4 slice. The times are simulated.
32 devices in a mesh: lat: 16 (over z, x, core), lon: 2 (over y).
Axes of the slice: x: 2, y: 2, z: 4, core: 2. Of those that a mesh axis runs over, the one named last changes fastest.
Arguments:
- field: bfloat16 [768, 3600, 128], P('lat', 'lon'), may hold values from -6 to 6
- spectral_weight: bfloat16 [64, 2, 128, 128], P('lon'), may hold values from -0.375 to 0.375
- conv_weight: bfloat16 [3, 3, 128, 128], replicated, may hold values from -0.1875 to 0.1875
- conv_bias: float32 [128], replicated, may hold values from -3 to 3
Outputs:
- block_out: bfloat16 [768, 3600, 128], P('lat', 'lon')
All inputs are finite; a program needn't handle non-finite values.
Results may differ from a plain program's by a relative error of at most 0.0052.
Values may be sent and summed in bfloat16 or wider, within the bound.
A program may use at most 832 MiB of HBM per device.

v0:
```python
import math

import jax
import jax.numpy as jnp
from jax import lax
from jax.sharding import PartitionSpec as P

M = 64
NLON = 3600


def with_halo(block, sides, width, periodic):
    for axis, dim in sides:
        count = lax.axis_size(axis)
        forward = [(i, i + 1) for i in range(count - 1)]
        if periodic:
            forward.append((count - 1, 0))
        backward = [(target, source) for source, target in forward]
        low = lax.ppermute(
            lax.slice_in_dim(block, block.shape[dim] - width, None, axis=dim), axis, forward
        )
        high = lax.ppermute(lax.slice_in_dim(block, 0, width, axis=dim), axis, backward)
        block = jnp.concatenate([low, block, high], axis=dim)
    return block


def forward_table(count, lon_start, lon_count):
    modes = jnp.arange(count, dtype=jnp.int32)[:, None]
    places = (jnp.arange(lon_count, dtype=jnp.int32) + lon_start)[None, :]
    phase_index = modes * places % NLON
    angle = phase_index.astype(jnp.float32) * (2.0 * math.pi / NLON)
    scale = 1.0 / math.sqrt(NLON)
    table = jnp.stack([jnp.cos(angle) * scale, -jnp.sin(angle) * scale], axis=1)
    return table.astype(jnp.bfloat16)


def inverse_table(count, lon_start, lon_count):
    modes = jnp.arange(count, dtype=jnp.int32)[:, None]
    places = (jnp.arange(lon_count, dtype=jnp.int32) + lon_start)[None, :]
    phase_index = modes * places % NLON
    angle = phase_index.astype(jnp.float32) * (2.0 * math.pi / NLON)
    weight = jnp.where(modes == 0, 1.0, 2.0).astype(jnp.float32) / math.sqrt(4.0 * M)
    table = jnp.stack([weight * jnp.cos(angle), -weight * jnp.sin(angle)], axis=1)
    return table.astype(jnp.bfloat16)


def mix_modes(spec_b, spectral_weight):
    w_real = spectral_weight[:, 0]
    w_imag = spectral_weight[:, 1]
    upper = jnp.concatenate([w_real, w_imag], axis=2)
    lower = jnp.concatenate([-w_imag, w_real], axis=2)
    block = jnp.concatenate([upper, lower], axis=1)
    joined = jnp.concatenate([spec_b[:, 0], spec_b[:, 1]], axis=2)
    product = jnp.einsum("mlc,mcd->mld", joined, block, preferred_element_type=jnp.float32)
    channels = spec_b.shape[3]
    stacked = jnp.stack([product[:, :, :channels], product[:, :, channels:]], axis=1)
    return stacked.astype(jnp.bfloat16)


def per_device(field, spectral_weight, conv_weight, conv_bias):
    lat_dev, lon_dev, channels = field.shape
    modes_local = spectral_weight.shape[0]
    lon_start = lax.axis_index("lon") * lon_dev
    table = forward_table(modes_local * lax.axis_size("lon"), lon_start, lon_dev)
    spectrum = lax.psum_scatter(
        jnp.einsum("mrn,lnc->mrlc", table, field, preferred_element_type=jnp.float32),
        "lon",
        scatter_dimension=0,
        tiled=True,
    )
    spec_b = spectrum.astype(jnp.bfloat16)
    mixed = mix_modes(spec_b, spectral_weight)
    piece = lax.all_gather(mixed, "lon", axis=0, tiled=True)
    table = inverse_table(piece.shape[0], lon_start, lon_dev)
    spectral = jnp.einsum("mrn,mrlc->lnc", table, piece, preferred_element_type=jnp.float32)
    widened = with_halo(field, (("lon", 1),), 1, True)
    padded = with_halo(widened, (("lat", 0),), 1, False)
    bypass = jnp.zeros((lat_dev, lon_dev, channels), jnp.float32)
    for i in range(3):
        for j in range(3):
            window = padded[i : i + lat_dev, j : j + lon_dev]
            bypass = bypass + jnp.dot(window, conv_weight[i, j], preferred_element_type=jnp.float32)
    return jax.nn.gelu(spectral + bypass + conv_bias).astype(jnp.bfloat16)


def solution(mesh):
    in_specs = (P("lat", "lon", None), P("lon", None, None, None), P(), P())
    out_specs = P("lat", "lon", None)
    return jax.shard_map(
        per_device, mesh=mesh, in_specs=in_specs, out_specs=out_specs, check_vma=False
    )
```

profile of v0, /device:TPU:1, one launch (start us, length us, event | category | flops | bytes accessed | tf_op | source)
XLA Modules:
  0.0 501.1 jit_solution(8015778101195616188)
XLA Ops:
  6.5 1.1 fusion.98
  7.7 2.1 collective-permute-start.1
  9.9 3.0 multiply_convert_fusion.1
  12.9 10.9 %fusion.33 = f32[64,2,48,128]{3,0,2,1:T(8,128)} fusion(bf16[48,1800,128]{2,1,0:T(8,128)(2,1)} %param.4, bf16[64,1,1800]{2,0,1:T(8,128)(2,1)S(1)} %get-tuple-element.17, bf16[64,1,1800]{2,0,1:T(8,128)(2,1)S(1)} %get-tuple-element.18), kind=kOutput, calls=%fused_computation.39 | convolution fusion | flops 2832076800 | bytes 25724928 | tf_op jit(solution)/shard_map/mrn,lnc->mrlc/dot_general | solution.py:66
  23.8 1.4 slice_bitcast_fusion
  25.3 24.6 %fusion.68 = f32[48,1800,128]{2,1,0:T(8,128)} fusion(bf16[48,1800,128]{2,1,0:T(8,128)(2,1)} %param.4, bf16[3,3,128,128]{3,2,1,0:T(8,128)(2,1)S(1)} %copy-done.9), kind=kOutput, calls=%fused_computation.88 | convolution fusion | flops 2831155200 | bytes 66387968 | tf_op jit(solution)/shard_map/dot_general | solution.py:82
  49.8 0.1 fusion.96
  50.0 107.6 %concatenate.36 = bf16[48,1802,128]{2,1,0:T(8,128)(2,1)} concatenate(bf16[48,1,128]{2,1,0:T(2,128)(2,1)S(1)} %collective-permute-done, bf16[48,1800,128]{2,1,0:T(8,128)(2,1)} %param.4, bf16[48,1,128]{2,1,0:T(2,128)(2,1)S(1)} %collective-permute-done.1), dimensions={1} | concatenate | bytes 44285952 | tf_op jit(solution)/shard_map/concatenate | solution.py:23
  157.6 1.2 fusion.97
  158.8 4.3 collective-permute-start.2
  163.2 2.1 collective-permute-start.3
  165.3 24.6 %fusion.25 = f32[48,1800,128]{2,1,0:T(8,128)} fusion(bf16[48,1,128]{2,1,0:T(2,128)(2,1)S(1)} %collective-permute-done.1, bf16[48,1800,128]{2,1,0:T(8,128)(2,1)} %param.4, bf16[3,3,128,128]{3,2,1,0:T(8,128)(2,1)S(1)} %copy-done.9), kind=kOutput, calls=%fused_computation.29 | convolution fusion | flops 2875392000 | bytes 66412544 | tf_op jit(solution)/shard_map/dot_general | solution.py:82
  189.9 24.6 %fusion.27 = f32[48,1800,128]{2,1,0:T(8,128)} fusion(bf16[48,1800,128]{2,1,0:T(8,128)(2,1)} %param.4, bf16[48,1,128]{2,1,0:T(2,128)(2,1)S(1)} %collective-permute-done, bf16[3,3,128,128]{3,2,1,0:T(8,128)(2,1)S(1)} %copy-done.9), kind=kOutput, calls=%fused_computation.32 | convolution fusion | flops 2875392000 | bytes 66412544 | tf_op jit(solution)/shard_map/dot_general | solution.py:82
  214.5 24.7 %fusion.13 = f32[48,1800,128]{2,1,0:T(8,128)} fusion(bf16[1,1802,128]{2,1,0:T(8,128)(2,1)S(1)} %collective-permute-done.3, bf16[48,1802,128]{2,1,0:T(8,128)(2,1)} %concatenate.36, bf16[3,3,128,128]{3,2,1,0:T(8,128)(2,1)S(1)} %copy-done.9), kind=kOutput, calls=%fused_computation.18 | convolution fusion | flops 2842214400 | bytes 66875392 | tf_op jit(solution)/shard_map/dot_general | solution.py:82
  239.2 24.8 %fusion.10 = f32[48,1800,128]{2,1,0:T(8,128)} fusion(bf16[1,1802,128]{2,1,0:T(8,128)(2,1)S(1)} %collective-permute-done.3, bf16[48,1802,128]{2,1,0:T(8,128)(2,1)} %concatenate.36, bf16[3,3,128,128]{3,2,1,0:T(8,128)(2,1)S(1)} %copy-done.9), kind=kOutput, calls=%fused_computation.16 | convolution fusion | flops 2842214400 | bytes 66875392 | tf_op jit(solution)/shard_map/dot_general | solution.py:82
  264.0 0.8 copy-done.5
  264.8 24.4 %fusion.19 = f32[48,1800,128]{2,1,0:T(8,128)} fusion(bf16[1,1802,128]{2,1,0:T(8,128)(2,1)S(1)} %collective-permute-done.2, bf16[48,1802,128]{2,1,0:T(8,128)(2,1)} %concatenate.36, bf16[3,3,128,128]{3,2,1,0:T(8,128)(2,1)S(1)} %copy-done.9), kind=kOutput, calls=%fused_computation.22 | convolution fusion | flops 2842214400 | bytes 66875392 | tf_op jit(solution)/shard_map/dot_general | solution.py:82
  289.2 1.6 convert_element_type.33
  291.0 1.5 fusion.49
  292.7 0.9 pad_maximum_fusion.11
  293.6 25.4 %fusion.16 = f32[48,1800,128]{2,1,0:T(8,128)} fusion(bf16[1,1802,128]{2,1,0:T(8,128)(2,1)} %copy-done.5, bf16[48,1802,128]{2,1,0:T(8,128)(2,1)} %concatenate.36, bf16[3,3,128,128]{3,2,1,0:T(8,128)(2,1)S(1)} %copy-done.9), kind=kOutput, calls=%fused_computation.20 | convolution fusion | flops 2842214400 | bytes 66873856 | tf_op jit(solution)/shard_map/dot_general | solution.py:82
  319.0 24.7 %fusion.29 = f32[48,1800,128]{2,1,0:T(8,128)} fusion(bf16[48,1802,128]{2,1,0:T(8,128)(2,1)} %concatenate.36, bf16[1,1802,128]{2,1,0:T(8,128)(2,1)S(1)} %copy-done.6, bf16[3,3,128,128]{3,2,1,0:T(8,128)(2,1)S(1)} %copy-done.9), kind=kOutput, calls=%fused_computation.35 | convolution fusion | flops 2875392000 | bytes 66875392 | tf_op jit(solution)/shard_map/dot_general | solution.py:82
  343.8 17.8 %fusion.47 = f32[48,128,1800,1]{1,2,3,0:T(8,128)} fusion(bf16[64,2,48,128]{3,2,0,1:T(8,128)(2,1)} %all-gather.2.cloned.1.call-done, bf16[64,1,1800]{2,0,1:T(8,128)(2,1)S(1)} %copy-done.4, bf16[64,1,1800]{2,0,1:T(8,128)(2,1)S(1)} %copy-done.3), kind=kOutput, calls=%fused_computation.53 | convolution fusion | flops 2831385600 | bytes 46270464 | tf_op jit(solution)/shard_map/mrn,mrlc->lnc/dot_general | solution.py:75
  361.5 132.2 %fusion.7 = bf16[48,1800,128]{2,1,0:T(8,128)(2,1)} fusion(f32[48,128,1800,1]{1,2,3,0:T(8,128)} %fusion.47, f32[48,1800,128]{2,1,0:T(8,128)} %fusion.10, f32[48,1800,128]{2,1,0:T(8,128)} %fusion.13, f32[48,1800,128]{2,1,0:T(8,128)} %fusion.25, f32[48,1800,128]{2,1,0:T(8,128)} %fusion.68, f32[48,1800,128]{2,1,0:T(8,128)} %fusion.27, ...), kind=kOutput, calls=%fused_computation.8 | convolution fusion | flops 3085516800 | bytes 442888704 | tf_op jit(solution)/shard_map/dot_general | solution.py:82
  (37 shorter events, 0.5 us)
Async XLA Ops:
  6.5 17.3 %copy-start = (bf16[32,2,128,128]{3,2,1,0:T(8,128)(2,1)S(1)}, bf16[32,2,128,128]{3,2,1,0:T(8,128)(2,1)}, u32[]{:S(2)}) copy-start(bf16[32,2,128,128]{3,2,1,0:T(8,128)(2,1)} %param.5) | copy-start | bytes 6291460
  6.5 18.7 %copy-start.9 = (bf16[3,3,128,128]{3,2,1,0:T(8,128)(2,1)S(1)}, bf16[3,3,128,128]{3,2,1,0:T(8,128)(2,1)}, u32[]{:S(2)}) copy-start(bf16[3,3,128,128]{3,2,1,0:T(8,128)(2,1)} %param.6) | copy-start | bytes 884740
  6.5 282.7 %reduce-scatter.2.cloned.1.call-start = ((), (), s32[]{:S(2)}) async-start(), calls=%async_computation.1 | async-start | bytes 4718592 | tf_op jit(solution)/shard_map/reduce_scatter | solution.py:65
  7.7 42.3 %collective-permute-start.1 = (bf16[48,1,128]{2,1,0:T(2,128)(2,1)S(1)}, bf16[48,1,128]{2,1,0:T(2,128)(2,1)S(1)}, u32[]{:S(2)}, u32[]{:S(2)}) collective-permute-start(bf16[48,1,128]{2,1,0:T(2,128)(2,1)S(1)} %get-tuple-element.7), channel_id=1, source_target_pairs={{1,0},{0,1},{3,2},{2,3},{5,4},{4,5},{7,6},{6,7},{9,8},{8,9},{11,10... | collective-permute-start | bytes 36872 | tf_op jit(solution)/shard_map/ppermute | solution.py:22
  9.8 40.2 %collective-permute-start = (bf16[48,1,128]{2,1,0:T(2,128)(2,1)S(1)}, bf16[48,1,128]{2,1,0:T(2,128)(2,1)S(1)}, u32[]{:S(2)}, u32[]{:S(2)}) collective-permute-start(bf16[48,1,128]{2,1,0:T(2,128)(2,1)S(1)} %get-tuple-element.8), channel_id=1, source_target_pairs={{0,1},{1,0},{2,3},{3,2},{4,5},{5,4},{6,7},{7,6},{8,9},{9,8},{10,11... | collective-permute-start | bytes 36872 | tf_op jit(solution)/shard_map/ppermute | solution.py:19
  23.8 320.0 %all-gather.2.cloned.1.call-start = ((), (), s32[]{:S(2)}) async-start(), calls=%async_computation.2 | async-start | bytes 2359296 | tf_op jit(solution)/shard_map/all_gather | solution.py:73
  158.8 105.1 %collective-permute-start.2 = (bf16[1,1802,128]{2,1,0:T(8,128)(2,1)S(1)}, bf16[1,1802,128]{2,1,0:T(8,128)(2,1)S(1)}, u32[]{:S(2)}, u32[]{:S(2)}) collective-permute-start(bf16[1,1802,128]{2,1,0:T(8,128)(2,1)S(1)} %get-tuple-element.5), channel_id=1, source_target_pairs={{0,2},{2,4},{4,6},{6,8},{8,10},{10,12},{12,14},{14,16},{16,18},{18... | collective-permute-start | bytes 1383944 | tf_op jit(solution)/shard_map/ppermute | solution.py:19
  163.2 51.3 %collective-permute-start.3 = (bf16[1,1802,128]{2,1,0:T(8,128)(2,1)S(1)}, bf16[1,1802,128]{2,1,0:T(8,128)(2,1)S(1)}, u32[]{:S(2)}, u32[]{:S(2)}) collective-permute-start(bf16[1,1802,128]{2,1,0:T(8,128)(2,1)S(1)} %get-tuple-element.6), channel_id=1, source_target_pairs={{2,0},{4,2},{6,4},{8,6},{10,8},{12,10},{14,12},{16,14},{18,16},{20... | collective-permute-start | bytes 1383944 | tf_op jit(solution)/shard_map/ppermute | solution.py:22
  214.5 24.7 %copy-start.7 = (bf16[1,1802,128]{2,1,0:T(8,128)(2,1)}, bf16[1,1802,128]{2,1,0:T(8,128)(2,1)S(1)}, u32[]{:S(2)}) copy-start(bf16[1,1802,128]{2,1,0:T(8,128)(2,1)S(1)} %collective-permute-done.3) | copy-start | bytes 1383940
  264.0 27.0 %copy-start.1 = (bf16[32,128,128]{2,1,0:T(8,128)(2,1)S(1)}, bf16[32,128,128]{2,1,0:T(8,128)(2,1)}, u32[]{:S(2)}) copy-start(bf16[32,128,128]{2,1,0:T(8,128)(2,1)} %get-tuple-element.9) | copy-start | bytes 3145732
  264.0 27.0 %copy-start.2 = (bf16[32,128,128]{2,1,0:T(8,128)(2,1)S(1)}, bf16[32,128,128]{2,1,0:T(8,128)(2,1)}, u32[]{:S(2)}) copy-start(bf16[32,128,128]{2,1,0:T(8,128)(2,1)} %get-tuple-element.10) | copy-start | bytes 3145732
  264.0 0.8 copy-start.5
  293.6 25.4 %copy-start.6 = (bf16[1,1802,128]{2,1,0:T(8,128)(2,1)S(1)}, bf16[1,1802,128]{2,1,0:T(8,128)(2,1)}, u32[]{:S(2)}) copy-start(bf16[1,1802,128]{2,1,0:T(8,128)(2,1)} %copy-done.5) | copy-start | bytes 1383940
  319.0 24.7 %copy-start.3 = (bf16[64,1,1800]{2,0,1:T(8,128)(2,1)S(1)}, bf16[64,1,1800]{2,0,1:T(8,128)(2,1)}, u32[]{:S(2)}) copy-start(bf16[64,1,1800]{2,0,1:T(8,128)(2,1)} %get-tuple-element.15) | copy-start | bytes 691204
  319.0 24.7 %copy-start.4 = (bf16[64,1,1800]{2,0,1:T(8,128)(2,1)S(1)}, bf16[64,1,1800]{2,0,1:T(8,128)(2,1)}, u32[]{:S(2)}) copy-start(bf16[64,1,1800]{2,0,1:T(8,128)(2,1)} %get-tuple-element.16) | copy-start | bytes 691204
  343.7 17.8 %copy-start.8 = (bf16[1,1802,128]{2,1,0:T(8,128)(2,1)S(1)}, bf16[1,1802,128]{2,1,0:T(8,128)(2,1)}, u32[]{:S(2)}) copy-start(bf16[1,1802,128]{2,1,0:T(8,128)(2,1)} %copy-done.7) | copy-start | bytes 1383940
  343.7 17.8 %copy-start.10 = (f32[128]{0:T(128)S(1)}, f32[128]{0:T(128)}, u32[]{:S(2)}) copy-start(f32[128]{0:T(128)} %param.7) | copy-start | bytes 1540
Sparse Core Ops, SparseCore 0:
  23.9 45.2 reduce-scatter.1
  293.7 28.4 all-gather.1
where the time goes:
time: 510 us; the launch traced here: 501 us
  matrix products  360 us (71%)
  local copies, waits for them, and re-layouts  112 us (22%)
  between operations  14.1 us (3%)
  starting transfers between devices  8.67 us (2%)
  other arithmetic  5.72 us (1%)
    dot_general x9, matrix products, per_device(): jnp.dot(window, conv_weight[i, j], preferred_element_type=jnp.float32)  330 us
    concatenate x1, local copies, waits for them, and re-layouts, with_halo(): block = jnp.concatenate([low, block, high], axis=dim)  108 us
    dot_general x1, matrix products, per_device(): jnp.einsum('mrn,mrlc->lnc', table, piece, preferred_element_type=jnp.floa...  17.8 us
    dot_general x1, matrix products, per_device(): jnp.einsum('mrn,lnc->mrlc', table, field, preferred_element_type=jnp.floa...  10.9 us
  transfers between devices with their start and end apart: 6, of which 0 were waited for; matrix products, arithmetic and copies ran while one was open for 64% of the time, Pallas kernels for 0%

commit v1 on v0

v1 whole, which is shorter than its diff:
```python
import functools
import math

import jax
import jax.numpy as jnp
import ml_dtypes
import numpy as np
from jax import lax
from jax.experimental import pallas as pl
from jax.experimental.pallas import tpu as pltpu
from jax.sharding import PartitionSpec as P

M = 64
NLON = 3600
TILE = 256
LAG = 16
VMEM = 56 * 1024 * 1024


def tables(shards, lon_dev, modes_local):
    angle = np.arange(NLON, dtype=np.float32) * np.float32(2.0 * math.pi / NLON)
    cos, sin = np.cos(angle), np.sin(angle)
    forward, inverse = [], []
    for index in range(shards):
        places = np.arange(lon_dev) + index * lon_dev

        def rows(step):
            owners = [(index + step * s) % shards for s in range(shards)]
            modes = np.concatenate([np.arange(modes_local) + o * modes_local for o in owners])
            return modes, modes[:, None] * places[None, :] % NLON

        modes, phase = rows(1)
        scale = np.float32(1.0 / math.sqrt(NLON))
        table = np.stack([cos[phase] * scale, -sin[phase] * scale], axis=1)
        forward.append(table.reshape(2 * len(modes), lon_dev))
        modes, phase = rows(-1)
        weight = (np.where(modes == 0, 1.0, 2.0) / math.sqrt(4.0 * M)).astype(np.float32)[:, None]
        table = np.stack([weight * cos[phase], -weight * sin[phase]], axis=1)
        inverse.append(table.reshape(2 * len(modes), lon_dev).T)
    return (
        np.stack(forward).astype(ml_dtypes.bfloat16),
        np.stack(inverse).astype(ml_dtypes.bfloat16),
    )


def dft_kernel(mine, index_ref, table_ref, x_ref, own_ref, send_ref):
    rows = x_ref.shape[0]
    channels = x_ref.shape[2]
    for l in range(0, rows, 2):
        pair = jnp.concatenate([x_ref[l], x_ref[l + 1]], axis=1)
        part = jnp.dot(table_ref[...], pair, preferred_element_type=jnp.float32)
        for d in range(2):
            half = part[:, d * channels : (d + 1) * channels]
            own_ref[l + d] = half[:mine]
            send_ref[l + d] = half[mine:].astype(jnp.bfloat16)


def forward_dft(index, field, table, mine):
    lat, lon, channels = field.shape
    rows = 8
    count = table.shape[1]
    return pl.pallas_call(
        functools.partial(dft_kernel, mine),
        grid_spec=pltpu.PrefetchScalarGridSpec(
            num_scalar_prefetch=1,
            grid=(lat // rows,),
            in_specs=[
                pl.BlockSpec((None, count, lon), lambda i, index: (index[0], 0, 0)),
                pl.BlockSpec((rows, lon, channels), lambda i, index: (i, 0, 0)),
            ],
            out_specs=[
                pl.BlockSpec((rows, mine, channels), lambda i, index: (i, 0, 0)),
                pl.BlockSpec((rows, count - mine, channels), lambda i, index: (i, 0, 0)),
            ],
        ),
        out_shape=[
            jax.ShapeDtypeStruct((lat, mine, channels), jnp.float32),
            jax.ShapeDtypeStruct((lat, count - mine, channels), jnp.bfloat16),
        ],
        compiler_params=pltpu.CompilerParams(vmem_limit_bytes=VMEM),
        cost_estimate=pl.CostEstimate(
            flops=2 * count * lat * lon * channels,
            bytes_accessed=2 * lat * lon * channels + 6 * lat * count * channels,
            transcendentals=0,
        ),
        name="forward_dft",
    )(index, table, field)


def mix_kernel(parts, own_ref, *refs):
    recv_refs, (w_ref, out_ref, s_ref, t_ref) = refs[:parts], refs[parts:]
    lat, mine, channels = own_ref.shape
    step = pl.program_id(0)
    group = w_ref.shape[0]

    @pl.when(step == 0)
    def _():
        total = own_ref[...]
        for recv_ref in recv_refs:
            total = total + recv_ref[...].astype(jnp.float32)
        s_ref[...] = total.reshape(lat * mine, channels)

    for g in range(group):
        m = step * group + g
        real = pl.ds(2 * m, lat, stride=mine)
        imag = pl.ds(2 * m + 1, lat, stride=mine)
        joined = jnp.concatenate(
            [s_ref[real, :].astype(jnp.bfloat16), s_ref[imag, :].astype(jnp.bfloat16)], axis=1
        )
        upper = jnp.concatenate([w_ref[g, 0], w_ref[g, 1]], axis=1)
        lower = jnp.concatenate([-w_ref[g, 1], w_ref[g, 0]], axis=1)
        block = jnp.concatenate([upper, lower], axis=0)
        product = jnp.dot(joined, block, preferred_element_type=jnp.float32)
        t_ref[real, :] = product[:, :channels]
        t_ref[imag, :] = product[:, channels:]

    @pl.when(step == pl.num_programs(0) - 1)
    def _():
        out_ref[...] = t_ref[...].reshape(lat, mine, channels).astype(jnp.bfloat16)


def mix_modes(own, received, spectral_weight):
    lat, mine, channels = own.shape
    modes = spectral_weight.shape[0]
    group = math.gcd(modes, 4)
    whole = pl.BlockSpec((lat, mine, channels), lambda i: (0, 0, 0))
    return pl.pallas_call(
        functools.partial(mix_kernel, len(received)),
        grid=(modes // group,),
        in_specs=[whole] * (1 + len(received))
        + [pl.BlockSpec((group, 2, channels, channels), lambda i: (i, 0, 0, 0))],
        out_specs=whole,
        out_shape=jax.ShapeDtypeStruct((lat, mine, channels), jnp.bfloat16),
        scratch_shapes=[pltpu.VMEM((lat * mine, channels), jnp.float32)] * 2,
        compiler_params=pltpu.CompilerParams(vmem_limit_bytes=VMEM),
        cost_estimate=pl.CostEstimate(
            flops=8 * modes * lat * channels * channels,
            bytes_accessed=4 * modes * channels * channels + 8 * lat * mine * channels,
            transcendentals=0,
        ),
        name="mix_modes",
    )(own, *received, spectral_weight)


def cuts(length):
    starts = list(range(0, max(length - TILE // 2, 1), TILE))
    return list(zip(starts, starts[1:] + [length]))


def convolve(a_ref, rows_ref, here, w_ref, low, high, channels, extra=None):
    lhs = jnp.concatenate([rows_ref[slot, low:high] for slot in here], axis=1)
    for j in range(3):
        result = jnp.dot(lhs, w_ref[j], preferred_element_type=jnp.float32)
        if j == 1 and extra is not None:
            result = result + jnp.dot(*extra, preferred_element_type=jnp.float32)
        for d in range(2):
            a_ref[j, d, 8 + low : 8 + high] = result[:, d * channels : (d + 1) * channels]


def taps(a_ref, d, low, size):
    return (
        a_ref[0, d, pl.ds(7 + low, size)]
        + a_ref[1, d, pl.ds(8 + low, size)]
        + a_ref[2, d, pl.ds(9 + low, size)]
    )


def stash_kernel(first, count, x_ref, w_ref, *refs):
    out_ref, rows_ref, a_ref, sems = refs[-4:]
    lon, channels = x_ref.shape[1:]
    step = pl.program_id(0)
    pair = first + step
    slots = rows_ref.shape[0]

    def fetch(place):
        slot = lax.rem(place, slots)
        return pltpu.make_async_copy(x_ref.at[place - 1], rows_ref.at[slot], sems.at[slot])

    @pl.when(step == 0)
    def _():
        for i in range(4):
            fetch(2 * pair + i).start()
        for i in range(2):
            fetch(2 * pair + i).wait()

    @pl.when(step + 1 < count)
    def _():
        for i in range(4, 6):
            fetch(2 * pair + i).start()

    for i in range(2, 4):
        fetch(2 * pair + i).wait()

    here = [lax.rem(2 * pair + i, slots) for i in range(4)]
    for d in range(2):
        a_ref[0, d, 7:8] = jnp.zeros((1, channels), jnp.float32)
        a_ref[2, d, 8 + lon : 9 + lon] = jnp.zeros((1, channels), jnp.float32)

    def finish(low, high):
        for d in range(2):
            out_ref[d, low:high] = taps(a_ref, d, low, high - low)

    done, ready = 0, 0
    for low, high in cuts(lon):
        convolve(a_ref, rows_ref, here, w_ref, low, high, channels)
        if ready > done:
            finish(done, ready)
            done = ready
        ready = high - LAG
    finish(done, lon)


def stash(field, weights, first, count, total, offset, before=None):
    lat, lon, channels = field.shape
    slots = 8
    extra = [] if before is None else [before]
    return pl.pallas_call(
        functools.partial(stash_kernel, first, count),
        grid=(count,),
        in_specs=[
            pl.BlockSpec(memory_space=pl.ANY),
            pl.BlockSpec(weights.shape, lambda i: (0, 0, 0)),
        ]
        + [pl.BlockSpec(memory_space=pl.ANY)] * len(extra),
        out_specs=pl.BlockSpec((2, lon, channels), lambda i: (i + offset, 0, 0)),
        out_shape=jax.ShapeDtypeStruct((2 * total, lon, channels), jnp.float32),
        input_output_aliases={2: 0} if extra else {},
        scratch_shapes=[
            pltpu.VMEM((slots, lon, channels), jnp.bfloat16),
            pltpu.VMEM((3, 2, (lon + 8) // 8 * 8 + 16, channels), jnp.float32),
            pltpu.SemaphoreType.DMA((slots,)),
        ],
        compiler_params=pltpu.CompilerParams(vmem_limit_bytes=VMEM),
        cost_estimate=pl.CostEstimate(
            flops=2 * 2 * count * lon * channels * 12 * channels,
            bytes_accessed=12 * count * lon * channels,
            transcendentals=0,
        ),
        name="stash",
    )(field, weights, *extra)


def block_kernel(
    stashed, pieces, index_ref, x_ref, halo_ref, stash_ref, w_ref, g_ref, edge_ref, bias_ref, *refs
):
    piece_refs, (out_ref, rows_ref, rhs_ref, a_ref, sems) = refs[:pieces], refs[pieces:]
    lat, lon, channels = x_ref.shape
    step = pl.program_id(0)
    slots = rows_ref.shape[0]
    last = lat // 2 - 1
    base = 1 + stashed
    wrap = lat + 2

    def virtual(at):
        return jnp.where(at == last, last + 2, at + 1)

    def fetch(source, place):
        slot = lax.rem(place, slots)
        return pltpu.make_async_copy(source, rows_ref.at[slot], sems.at[slot])

    def start(place):
        real = jnp.where(place >= wrap, place - wrap, place)

        @pl.when(real == 0)
        def _():
            fetch(halo_ref.at[0], place).start()

        @pl.when(real == lat + 1)
        def _():
            fetch(halo_ref.at[1], place).start()

        @pl.when(jnp.logical_and(real > 0, real < lat + 1))
        def _():
            fetch(x_ref.at[jnp.clip(real - 1, 0, lat - 1)], place).start()

    def wait(place):
        fetch(halo_ref.at[0], place).wait()

    def fresh(pair):
        return jnp.logical_or(pair == base, pair == last + 2)

    def begin(at):
        pair = virtual(at)

        @pl.when(fresh(pair))
        def _():
            start(2 * pair)
            start(2 * pair + 1)

        @pl.when(pair >= base)
        def _():
            start(2 * pair + 2)
            start(2 * pair + 3)

    if stashed == 0:
        @pl.when(step == 0)
        def _():
            begin(step)

    @pl.when(step < last)
    def _():
        begin(step + 1)

    top = 0
    for piece_ref in piece_refs:
        size = piece_ref.shape[1]
        for d in range(2):
            rhs_ref[top : top + size, d * channels : (d + 1) * channels] = piece_ref[d]
        top += size
    bias = bias_ref[...]
    c1 = math.sqrt(2.0 / math.pi)
    c2 = c1 * 0.044715

    def gelu(x):
        t = jnp.tanh(x * (c1 + c2 * (x * x)))
        return (x * (0.5 + 0.5 * t)).astype(jnp.bfloat16)

    pair = virtual(step)

    @pl.when(pair < base)
    def _():
        for low, high in cuts(lon):
            part = jnp.dot(g_ref[low:high], rhs_ref[...], preferred_element_type=jnp.float32)
            for d in range(2):
                x = part[:, d * channels : (d + 1) * channels] + stash_ref[d, low:high] + bias
                place = low + lax.broadcasted_iota(jnp.int32, x.shape, 0)
                if low == 0:
                    x = x + jnp.where(place == 0, edge_ref[d, 0:1], 0.0)
                if high == lon:
                    x = x + jnp.where(place == lon - 1, edge_ref[d, 1:2], 0.0)
                out_ref[d, low:high] = gelu(x)

    @pl.when(pair >= base)
    def _():
        @pl.when(fresh(pair))
        def _():
            wait(2 * pair)
            wait(2 * pair + 1)

        wait(2 * pair + 2)
        wait(2 * pair + 3)
        here = [lax.rem(2 * pair + i, slots) for i in range(4)]
        for d in range(2):
            a_ref[0, d, 7:8] = edge_ref[d, 0:1]
            a_ref[2, d, 8 + lon : 9 + lon] = edge_ref[d, 1:2]

        def finish(low, high):
            for d in range(2):
                out_ref[d, low:high] = gelu(taps(a_ref, d, low, high - low) + bias)

        done, ready = 0, 0
        for low, high in cuts(lon):
            extra = (g_ref[low:high], rhs_ref[...])
            convolve(a_ref, rows_ref, here, w_ref, low, high, channels, extra)
            if ready > done:
                finish(done, ready)
                done = ready
            ready = high - LAG
        finish(done, lon)


def block(index, field, halo, stashed, weights, table, edges, bias, pieces):
    lat, lon, channels = field.shape
    count = table.shape[2]
    slots = 8
    pairs = lat // 2
    held = stashed.shape[0] // 2

    def pair(i, index):
        return (lax.rem(i + 1, pairs), 0, 0)

    return pl.pallas_call(
        functools.partial(block_kernel, held, len(pieces)),
        grid_spec=pltpu.PrefetchScalarGridSpec(
            num_scalar_prefetch=1,
            grid=(pairs,),
            in_specs=[
                pl.BlockSpec(memory_space=pl.ANY),
                pl.BlockSpec(memory_space=pl.ANY),
                pl.BlockSpec(
                    (2, lon, channels), lambda i, index: (jnp.minimum(i, held - 1), 0, 0)
                ),
                pl.BlockSpec(weights.shape, lambda i, index: (0, 0, 0)),
                pl.BlockSpec((None, lon, count), lambda i, index: (index[0], 0, 0)),
                pl.BlockSpec((2, 2, channels), pair),
                pl.BlockSpec((1, channels), lambda i, index: (0, 0)),
            ]
            + [pl.BlockSpec((2, p.shape[1], channels), pair) for p in pieces],
            out_specs=pl.BlockSpec((2, lon, channels), pair),
            scratch_shapes=[
                pltpu.VMEM((slots, lon, channels), jnp.bfloat16),
                pltpu.VMEM((count, 2 * channels), jnp.bfloat16),
                pltpu.VMEM((3, 2, (lon + 8) // 8 * 8 + 16, channels), jnp.float32),
                pltpu.SemaphoreType.DMA((slots,)),
            ],
        ),
        out_shape=jax.ShapeDtypeStruct((lat, lon, channels), jnp.bfloat16),
        compiler_params=pltpu.CompilerParams(vmem_limit_bytes=VMEM),
        cost_estimate=pl.CostEstimate(
            flops=2 * lat * lon * channels * (9 * channels + count),
            bytes_accessed=4 * lat * lon * channels,
            transcendentals=lat * lon * channels,
        ),
        name="block",
    )(index, field, halo, stashed, weights, table, edges, bias, *pieces)


def shift(x, axis, by, periodic=True):
    count = lax.axis_size(axis)
    pairs = [(i, (i + by) % count) for i in range(count) if periodic or 0 <= i + by < count]
    return lax.ppermute(x, axis, pairs)


def pair_weights(conv_weight):
    zero = jnp.zeros_like(conv_weight[0, 0])
    return jnp.stack(
        [
            jnp.concatenate(
                [
                    jnp.concatenate([conv_weight[i, j] if i < 3 else zero for i in range(4)], axis=0),
                    jnp.concatenate([conv_weight[i - 1, j] if i else zero for i in range(4)], axis=0),
                ],
                axis=1,
            )
            for j in range(3)
        ]
    )


def per_device(field, spectral_weight, conv_weight, conv_bias):
    lat, lon, channels = field.shape
    modes_local = spectral_weight.shape[0]
    shards = lax.axis_size("lon")
    index = lax.axis_index("lon")
    mine = 2 * modes_local
    forward, inverse = tables(shards, lon, modes_local)
    index = index.astype(jnp.int32)[None]
    weights = pair_weights(conv_weight)

    own, send = forward_dft(index, field, jnp.asarray(forward), mine)
    received = [shift(send[:, (s - 1) * mine : s * mine], "lon", s) for s in range(1, shards)]

    outer = (field[lat - 1 :], field[:1], field[:, lon - 1], field[:, 0], weights)
    outer, send = lax.optimization_barrier((outer, send))
    low_row, high_row, east_column, west_column, weights = outer
    above = shift(low_row, "lat", 1, False)
    below = shift(high_row, "lat", -1, False)
    easts = jnp.concatenate([above[:, lon - 1], east_column, below[:, lon - 1]], axis=0)
    wests = jnp.concatenate([above[:, 0], west_column, below[:, 0]], axis=0)
    if shards == 2:
        columns = shift(jnp.stack([easts, wests], axis=1), "lon", 1)
    else:
        columns = jnp.stack([shift(easts, "lon", 1), shift(wests, "lon", -1)], axis=1)
    edges = jnp.stack(
        [
            sum(
                jnp.dot(
                    columns[i : i + lat, side],
                    conv_weight[i, 2 * side],
                    preferred_element_type=jnp.float32,
                )
                for i in range(3)
            )
            for side in range(2)
        ],
        axis=1,
    )
    halo = jnp.concatenate([above, below], axis=0)

    first, second = lat // 12, 7 * lat // 48
    total = first + second
    held = stash(field, weights, 1, first, total, 0)
    held, received = lax.optimization_barrier((held, received))
    mixed = mix_modes(own, received, spectral_weight)
    held, mixed = lax.optimization_barrier((held, mixed))
    pieces = [mixed] + [shift(mixed, "lon", s) for s in range(1, shards)]
    held = stash(field, weights, 1 + first, second, total, first, held)
    held, edges, halo = lax.optimization_barrier((held, edges, halo))
    return block(
        index, field, halo, held, weights, jnp.asarray(inverse), edges, conv_bias[None, :], pieces
    )


def solution(mesh):
    in_specs = (P("lat", "lon", None), P("lon", None, None, None), P(), P())
    out_specs = P("lat", "lon", None)
    return jax.shard_map(
        per_device, mesh=mesh, in_specs=in_specs, out_specs=out_specs, check_vma=False
    )
```

time: 510 us -> 114 us (0.22); the launches traced: 501 us -> 113 us
  matrix products: 360 us -> 0.81 us
  local copies, waits for them, and re-layouts: 112 us -> 4.01 us
  Pallas kernels: 0 us -> 94.1 us
  between operations: 14.1 us -> 0.15 us
    dot_general x12 -> x6, matrix products: 360 us -> 0.81 us  [per_device(): jnp.dot(columns[i:i + lat, side], conv_weight[i, 2 * side], preferred_ele...]
    concatenate x1 -> x0, local copies, waits for them, and re-layouts: 108 us -> none  [with_halo(): block = jnp.concatenate([low, block, high], axis=dim)]
    pallas_call x0 -> x5, Pallas kernels: none -> 94.1 us  [the longest x1 46.5 us: block(): pl.pallas_call(functools.partial(block_kernel, held, len(pieces)), grid_s...]
  transfers between devices with their start and end apart: 6 -> 5, of which waited for: 0 -> 2; matrix products, arithmetic and copies ran while one was open for 64% -> 5% of each run, Pallas kernels for 0% -> 26%
where the time goes in v1:
time: 114 us; the launch traced here: 113 us
  Pallas kernels  94.1 us (83%)
  starting transfers between devices  8.45 us (7%)
  local copies, waits for them, and re-layouts  4.01 us (4%)
  other arithmetic  2.75 us (2%)
  waiting for transfers between devices  2.68 us (2%)
    pallas_call x1, Pallas kernels, block(): pl.pallas_call(functools.partial(block_kernel, held, len(pieces)), grid_s...  46.5 us
    pallas_call x2, Pallas kernels, stash(): pl.pallas_call(functools.partial(stash_kernel, first, count), grid=(count...  29.3 us
    pallas_call x1, Pallas kernels, forward_dft(): pl.pallas_call(functools.partial(dft_kernel, mine), grid_spec=pltpu.Prefe...  11.1 us
    ppermute x5, starting transfers between devices, shift(): return lax.ppermute(x, axis, pairs)  8.45 us
    pallas_call x1, Pallas kernels, mix_modes(): pl.pallas_call(functools.partial(mix_kernel, len(received)), grid=(modes...  7.23 us
    ppermute x5, waiting for transfers between devices, shift(): return lax.ppermute(x, axis, pairs)  2.68 us
  transfers between devices with their start and end apart: 5, of which 2 were waited for; matrix products, arithmetic and copies ran while one was open for 5% of the time, Pallas kernels for 26%

profile of v1, /device:TPU:1, one launch (start us, length us, event | category | flops | bytes accessed | tf_op | source)
XLA Modules:
  0.0 113.0 jit_solution(15981981746513968874)
XLA Ops:
  0.0 11.1 %forward_dft.1 = (f32[48,64,128]{2,1,0:T(8,128)}, bf16[48,64,128]{2,1,0:T(8,128)(2,1)}) custom-call(s32[1]{0:T(128)} %bitcast.index_ref, bf16[2,128,1800]{2,1,0:T(8,128)(2,1)} %constant.10.clone.table_ref, bf16[48,1800,128]{2,1,0:T(8,128)(2,1)} %x_ref.7), custom_call_target="tpu_custom_call" | custom-call | flops 2831155200 | bytes 26836992 | tf_op jit(solution)/shard_map/forward_dft/pallas_call | solution.py:62
  11.1 2.1 %collective-permute-start = (bf16[48,64,128]{2,1,0:T(8,128)(2,1)}, bf16[48,64,128]{2,1,0:T(8,128)(2,1)S(1)}, u32[]{:S(2)}, u32[]{:S(2)}) collective-permute-start(bf16[48,64,128]{2,1,0:T(8,128)(2,1)} %get-tuple-element.19), channel_id=1, source_target_pairs={{0,1},{1,0},{2,3},{3,2},{4,5},{5,4},{6,7},{7,6},{8,9},{9,8},{10,11... | collective-permute-start | bytes 2359304 | tf_op jit(solution)/shard_map/ppermute | solution.py:411
  13.2 1.0 fusion.18
  14.2 1.2 %fusion.19 = (bf16[1,1800,128]{2,1,0:T(8,128)(2,1)S(1)}, bf16[1,1800,128]{2,1,0:T(8,128)(2,1)S(1)}) fusion(bf16[48,1800,128]{2,1,0:T(8,128)(2,1)} %x_ref.7), kind=kLoop, calls=%fused_computation.54 | loop fusion | bytes 1843200 | tf_op jit(solution)/shard_map/slice | solution.py:443
  15.5 1.0 pad_maximum_fusion.1.w_ref
  16.5 3.9 %collective-permute-start.1 = (bf16[1,1800,128]{2,1,0:T(8,128)(2,1)S(1)}, bf16[1,1800,128]{2,1,0:T(8,128)(2,1)S(1)}, u32[]{:S(2)}, u32[]{:S(2)}) collective-permute-start(bf16[1,1800,128]{2,1,0:T(8,128)(2,1)S(1)} %get-tuple-element.25), channel_id=1, source_target_pairs={{0,2},{2,4},{4,6},{6,8},{8,10},{10,12},{12,14},{14,16},{16,18},{18... | collective-permute-start | bytes 1382408 | tf_op jit(solution)/shard_map/ppermute | solution.py:411
  20.5 1.9 %collective-permute-start.2 = (bf16[1,1800,128]{2,1,0:T(8,128)(2,1)S(1)}, bf16[1,1800,128]{2,1,0:T(8,128)(2,1)S(1)}, u32[]{:S(2)}, u32[]{:S(2)}) collective-permute-start(bf16[1,1800,128]{2,1,0:T(8,128)(2,1)S(1)} %get-tuple-element.27), channel_id=1, source_target_pairs={{2,0},{4,2},{6,4},{8,6},{10,8},{12,10},{14,12},{16,14},{18,16},{20... | collective-permute-start | bytes 1382408 | tf_op jit(solution)/shard_map/ppermute | solution.py:411
  22.4 11.7 %stash.2.refs_0_ = f32[22,1800,128]{2,1,0:T(8,128)} custom-call(bf16[48,1800,128]{2,1,0:T(8,128)(2,1)} %x_ref.7, bf16[3,512,256]{2,1,0:T(8,128)(2,1)} %pad_maximum_fusion.1.w_ref), custom_call_target="tpu_custom_call" | custom-call | flops 5662310400 | bytes 11059200 | tf_op jit(solution)/shard_map/stash/pallas_call | solution.py:217
  34.2 0.3 collective-permute-start.3
  34.5 1.0 pad_maximum_fusion.halo_ref
  35.5 1.5 %collective-permute-done.3 = bf16[50,2,128]{2,0,1:T(8,128)(2,1)S(1)} collective-permute-done((bf16[50,2,128]{2,0,1:T(8,128)(2,1)S(1)}, bf16[50,2,128]{2,0,1:T(8,128)(2,1)S(1)}, u32[]{:S(2)}, u32[]{:S(2)}) %collective-permute-start.3) | collective-permute-done | bytes 25632 | tf_op jit(solution)/shard_map/ppermute | solution.py:411
  37.1 0.1 fusion.15
  37.3 0.1 fusion.16
  37.4 0.1 fusion.17
  37.5 0.1 fusion
  37.7 0.1 fusion.1
  37.8 0.7 pad_maximum_fusion.8.edge_ref
  38.5 0.9 copy-done.1
  39.4 7.2 %mix_modes.1.refs_0_ = bf16[48,64,128]{2,1,0:T(8,128)(2,1)} custom-call(f32[48,64,128]{2,1,0:T(8,128)} %get-tuple-element.22.own_ref, bf16[48,64,128]{2,1,0:T(8,128)(2,1)} %copy-done.1, bf16[32,2,128,128]{3,2,1,0:T(8,128)(2,1)} %refs_1_.1), custom_call_target="tpu_custom_call" | custom-call | flops 201326592 | bytes 5242880 | tf_op jit(solution)/shard_map/mix_modes/pallas_call | solution.py:127
  46.6 0.2 collective-permute-start.4
  46.8 17.6 %stash.3.stash_ref = f32[22,1800,128]{2,1,0:T(8,128)} custom-call(bf16[48,1800,128]{2,1,0:T(8,128)(2,1)} %x_ref.7, bf16[3,512,256]{2,1,0:T(8,128)(2,1)} %pad_maximum_fusion.1.w_ref, f32[22,1800,128]{2,1,0:T(8,128)} %stash.2.refs_0_), custom_call_target="tpu_custom_call", output_to_operand_aliasing={{}: (2, {})} | custom-call | flops 9909043200 | bytes 19353600 | tf_op jit(solution)/shard_map/stash/pallas_call | solution.py:217
  64.4 1.2 %collective-permute-done.4.refs_1_ = bf16[48,64,128]{2,1,0:T(8,128)(2,1)S(1)} collective-permute-done((bf16[48,64,128]{2,1,0:T(8,128)(2,1)}, bf16[48,64,128]{2,1,0:T(8,128)(2,1)S(1)}, u32[]{:S(2)}, u32[]{:S(2)}) %collective-permute-start.4) | collective-permute-done | bytes 786464 | tf_op jit(solution)/shard_map/ppermute | solution.py:411
  65.6 0.9 copy-done.2
  66.4 46.5 %block.1 = bf16[48,1800,128]{2,1,0:T(8,128)(2,1)} custom-call(s32[1]{0:T(128)} %bitcast.index_ref, bf16[48,1800,128]{2,1,0:T(8,128)(2,1)} %x_ref.7, bf16[2,1800,128]{2,1,0:T(8,128)(2,1)} %pad_maximum_fusion.halo_ref, f32[22,1800,128]{2,1,0:T(8,128)} %stash.3.stash_ref, bf16[3,512,256]{2,1,0:T(8,128)(2,1)} %pad_maximum_fusion.1.w_ref, ...), custom_call_target="tpu_custom_call" | custom-call | flops 28311552000 | bytes 44236800 | tf_op jit(solution)/shard_map/block/pallas_call | solution.py:372
  (18 shorter events, 0.3 us)
Async XLA Ops:
  0.0 15.4 %copy-start = (bf16[3,3,128,128]{3,2,1,0:T(8,128)(2,1)S(1)}, bf16[3,3,128,128]{3,2,1,0:T(8,128)(2,1)}, u32[]{:S(2)}) copy-start(bf16[3,3,128,128]{3,2,1,0:T(8,128)(2,1)} %param.8) | copy-start | bytes 884740
  11.1 27.4 %collective-permute-start = (bf16[48,64,128]{2,1,0:T(8,128)(2,1)}, bf16[48,64,128]{2,1,0:T(8,128)(2,1)S(1)}, u32[]{:S(2)}, u32[]{:S(2)}) collective-permute-start(bf16[48,64,128]{2,1,0:T(8,128)(2,1)} %get-tuple-element.19), channel_id=1, source_target_pairs={{0,1},{1,0},{2,3},{3,2},{4,5},{5,4},{6,7},{7,6},{8,9},{9,8},{10,11... | collective-permute-start | bytes 2359304 | tf_op jit(solution)/shard_map/ppermute | solution.py:411
  16.5 17.6 %collective-permute-start.1 = (bf16[1,1800,128]{2,1,0:T(8,128)(2,1)S(1)}, bf16[1,1800,128]{2,1,0:T(8,128)(2,1)S(1)}, u32[]{:S(2)}, u32[]{:S(2)}) collective-permute-start(bf16[1,1800,128]{2,1,0:T(8,128)(2,1)S(1)} %get-tuple-element.25), channel_id=1, source_target_pairs={{0,2},{2,4},{4,6},{6,8},{8,10},{10,12},{12,14},{14,16},{16,18},{18... | collective-permute-start | bytes 1382408 | tf_op jit(solution)/shard_map/ppermute | solution.py:411
  20.5 13.7 %collective-permute-start.2 = (bf16[1,1800,128]{2,1,0:T(8,128)(2,1)S(1)}, bf16[1,1800,128]{2,1,0:T(8,128)(2,1)S(1)}, u32[]{:S(2)}, u32[]{:S(2)}) collective-permute-start(bf16[1,1800,128]{2,1,0:T(8,128)(2,1)S(1)} %get-tuple-element.27), channel_id=1, source_target_pairs={{2,0},{4,2},{6,4},{8,6},{10,8},{12,10},{14,12},{16,14},{18,16},{20... | collective-permute-start | bytes 1382408 | tf_op jit(solution)/shard_map/ppermute | solution.py:411
  34.2 2.8 %collective-permute-start.3 = (bf16[50,2,128]{2,0,1:T(8,128)(2,1)S(1)}, bf16[50,2,128]{2,0,1:T(8,128)(2,1)S(1)}, u32[]{:S(2)}, u32[]{:S(2)}) collective-permute-start(bf16[50,2,128]{2,0,1:T(8,128)(2,1)S(1)} %pad_maximum_fusion.9), channel_id=1, source_target_pairs={{0,1},{1,0},{2,3},{3,2},{4,5},{5,4},{6,7},{7,6},{8,9},{9,8},{10,11... | collective-permute-start | bytes 76808 | tf_op jit(solution)/shard_map/ppermute | solution.py:411
  38.5 0.9 copy-start.1
  46.6 19.0 %collective-permute-start.4 = (bf16[48,64,128]{2,1,0:T(8,128)(2,1)}, bf16[48,64,128]{2,1,0:T(8,128)(2,1)S(1)}, u32[]{:S(2)}, u32[]{:S(2)}) collective-permute-start(bf16[48,64,128]{2,1,0:T(8,128)(2,1)} %mix_modes.1.refs_0_), channel_id=1, source_target_pairs={{0,1},{1,0},{2,3},{3,2},{4,5},{5,4},{6,7},{7,6},{8,9},{9,8},{10,11... | collective-permute-start | bytes 2359304 | tf_op jit(solution)/shard_map/ppermute | solution.py:411
  65.6 0.9 copy-start.2

commit v2 on v1

--- a/solution.py
+++ b/solution.py
@@ -12,7 +12,7 @@
 
 M = 64
 NLON = 3600
-TILE = 256
+TILE = 512
 LAG = 16
 VMEM = 56 * 1024 * 1024
 
@@ -43,11 +43,12 @@
     )
 
 
-def dft_kernel(mine, index_ref, table_ref, x_ref, own_ref, send_ref):
-    rows = x_ref.shape[0]
-    channels = x_ref.shape[2]
-    for l in range(0, rows, 2):
-        pair = jnp.concatenate([x_ref[l], x_ref[l + 1]], axis=1)
+def dft_kernel(mine, index_ref, table_ref, *refs):
+    x_refs, (own_ref, send_ref) = refs[:-2], refs[-2:]
+    channels = own_ref.shape[2]
+    for n, x_ref in enumerate(x_refs):
+        l = 2 * n
+        pair = jnp.concatenate([x_ref[0], x_ref[1]], axis=1)
         part = jnp.dot(table_ref[...], pair, preferred_element_type=jnp.float32)
         for d in range(2):
             half = part[:, d * channels : (d + 1) * channels]
@@ -57,7 +58,8 @@
 
 def forward_dft(index, field, table, mine):
     lat, lon, channels = field.shape
-    rows = 8
+    streams = 4
+    rows = 2 * streams
     count = table.shape[1]
     return pl.pallas_call(
         functools.partial(dft_kernel, mine),
@@ -66,7 +68,12 @@
             grid=(lat // rows,),
             in_specs=[
                 pl.BlockSpec((None, count, lon), lambda i, index: (index[0], 0, 0)),
-                pl.BlockSpec((rows, lon, channels), lambda i, index: (i, 0, 0)),
+            ]
+            + [
+                pl.BlockSpec(
+                    (2, lon, channels), functools.partial(lambda n, i, index: (streams * i + n, 0, 0), n)
+                )
+                for n in range(streams)
             ],
             out_specs=[
                 pl.BlockSpec((rows, mine, channels), lambda i, index: (i, 0, 0)),
@@ -84,7 +91,7 @@
             transcendentals=0,
         ),
         name="forward_dft",
-    )(index, table, field)
+    )(index, table, *[field] * streams)
 
 
 def mix_kernel(parts, own_ref, *refs):
@@ -122,7 +129,7 @@
 def mix_modes(own, received, spectral_weight):
     lat, mine, channels = own.shape
     modes = spectral_weight.shape[0]
-    group = math.gcd(modes, 4)
+    group = math.gcd(modes, 8)
     whole = pl.BlockSpec((lat, mine, channels), lambda i: (0, 0, 0))
     return pl.pallas_call(
         functools.partial(mix_kernel, len(received)),
@@ -198,7 +205,7 @@
 
     def finish(low, high):
         for d in range(2):
-            out_ref[d, low:high] = taps(a_ref, d, low, high - low)
+            out_ref[d, low:high] = taps(a_ref, d, low, high - low).astype(jnp.bfloat16)
 
     done, ready = 0, 0
     for low, high in cuts(lon):
@@ -223,7 +230,7 @@
         ]
         + [pl.BlockSpec(memory_space=pl.ANY)] * len(extra),
         out_specs=pl.BlockSpec((2, lon, channels), lambda i: (i + offset, 0, 0)),
-        out_shape=jax.ShapeDtypeStruct((2 * total, lon, channels), jnp.float32),
+        out_shape=jax.ShapeDtypeStruct((2 * total, lon, channels), jnp.bfloat16),
         input_output_aliases={2: 0} if extra else {},
         scratch_shapes=[
             pltpu.VMEM((slots, lon, channels), jnp.bfloat16),
@@ -233,7 +240,7 @@
         compiler_params=pltpu.CompilerParams(vmem_limit_bytes=VMEM),
         cost_estimate=pl.CostEstimate(
             flops=2 * 2 * count * lon * channels * 12 * channels,
-            bytes_accessed=12 * count * lon * channels,
+            bytes_accessed=8 * count * lon * channels,
             transcendentals=0,
         ),
         name="stash",
@@ -322,7 +329,8 @@
         for low, high in cuts(lon):
             part = jnp.dot(g_ref[low:high], rhs_ref[...], preferred_element_type=jnp.float32)
             for d in range(2):
-                x = part[:, d * channels : (d + 1) * channels] + stash_ref[d, low:high] + bias
+                x = part[:, d * channels : (d + 1) * channels] + stash_ref[d, low:high].astype(jnp.float32)
+                x = x + bias
                 place = low + lax.broadcasted_iota(jnp.int32, x.shape, 0)
                 if low == 0:
                     x = x + jnp.where(place == 0, edge_ref[d, 0:1], 0.0)

time: 114 us -> 110 us (0.965)
  Pallas kernels: 94.1 us -> 88.9 us
    pallas_call x1, Pallas kernels: 46.5 us -> 44.3 us  [block(): pl.pallas_call(functools.partial(block_kernel, held, len(pieces)), grid_s...]
    pallas_call x1, Pallas kernels: 7.23 us -> 5.53 us  [mix_modes(): pl.pallas_call(functools.partial(mix_kernel, len(received)), grid=(modes...]
    pallas_call x2, Pallas kernels: 29.3 us -> 27.8 us  [stash(): pl.pallas_call(functools.partial(stash_kernel, first, count), grid=(count...]
where the time goes in v2:
time: 110 us; the launch traced here: 109 us
  Pallas kernels  88.9 us (81%)
  starting transfers between devices  8.43 us (8%)
  local copies, waits for them, and re-layouts  4.17 us (4%)
  waiting for transfers between devices  3.52 us (3%)
  other arithmetic  2.73 us (2%)
    pallas_call x1, Pallas kernels, block(): pl.pallas_call(functools.partial(block_kernel, held, len(pieces)), grid_s...  44.3 us
    pallas_call x2, Pallas kernels, stash(): pl.pallas_call(functools.partial(stash_kernel, first, count), grid=(count...  27.8 us
    pallas_call x1, Pallas kernels, forward_dft(): pl.pallas_call(functools.partial(dft_kernel, mine), grid_spec=pltpu.Prefe...  11.3 us
    ppermute x5, starting transfers between devices, shift(): return lax.ppermute(x, axis, pairs)  8.43 us
    pallas_call x1, Pallas kernels, mix_modes(): pl.pallas_call(functools.partial(mix_kernel, len(received)), grid=(modes...  5.53 us
    ppermute x5, waiting for transfers between devices, shift(): return lax.ppermute(x, axis, pairs)  3.52 us
  transfers between devices with their start and end apart: 5, of which 2 were waited for; matrix products, arithmetic and copies ran while one was open for 5% of the time, Pallas kernels for 26%

profile of v2, /device:TPU:1, one launch (start us, length us, event | category | flops | bytes accessed | tf_op | source)
XLA Modules:
  0.0 108.7 jit_solution(49411437947514826)
XLA Ops:
  0.0 11.3 %forward_dft.1 = (f32[48,64,128]{2,1,0:T(8,128)}, bf16[48,64,128]{2,1,0:T(8,128)(2,1)}) custom-call(s32[1]{0:T(128)} %bitcast.index_ref, bf16[2,128,1800]{2,1,0:T(8,128)(2,1)} %constant.10.clone.table_ref, bf16[48,1800,128]{2,1,0:T(8,128)(2,1)} %x_ref.5, bf16[48,1800,128]{2,1,0:T(8,128)(2,1)} %x_ref.5, bf16[48,1800,128]{2,1,0:T(8,128)(2,1)} %x_ref.5, ...), custom_call_target="tpu_custom_call" | custom-call | flops 2831155200 | bytes 26836992 | tf_op jit(solution)/shard_map/forward_dft/pallas_call | solution.py:64
  11.3 2.1 %collective-permute-start = (bf16[48,64,128]{2,1,0:T(8,128)(2,1)}, bf16[48,64,128]{2,1,0:T(8,128)(2,1)S(1)}, u32[]{:S(2)}, u32[]{:S(2)}) collective-permute-start(bf16[48,64,128]{2,1,0:T(8,128)(2,1)} %get-tuple-element.19), channel_id=1, source_target_pairs={{0,1},{1,0},{2,3},{3,2},{4,5},{5,4},{6,7},{7,6},{8,9},{9,8},{10,11... | collective-permute-start | bytes 2359304 | tf_op jit(solution)/shard_map/ppermute | solution.py:419
  13.3 1.0 fusion.18
  14.3 1.2 %fusion.19 = (bf16[1,1800,128]{2,1,0:T(8,128)(2,1)S(1)}, bf16[1,1800,128]{2,1,0:T(8,128)(2,1)S(1)}) fusion(bf16[48,1800,128]{2,1,0:T(8,128)(2,1)} %x_ref.5), kind=kLoop, calls=%fused_computation.54 | loop fusion | bytes 1843200 | tf_op jit(solution)/shard_map/slice | solution.py:451
  15.7 1.0 pad_maximum_fusion.1.w_ref
  16.6 4.0 %collective-permute-start.1 = (bf16[1,1800,128]{2,1,0:T(8,128)(2,1)S(1)}, bf16[1,1800,128]{2,1,0:T(8,128)(2,1)S(1)}, u32[]{:S(2)}, u32[]{:S(2)}) collective-permute-start(bf16[1,1800,128]{2,1,0:T(8,128)(2,1)S(1)} %get-tuple-element.25), channel_id=1, source_target_pairs={{0,2},{2,4},{4,6},{6,8},{8,10},{10,12},{12,14},{14,16},{16,18},{18... | collective-permute-start | bytes 1382408 | tf_op jit(solution)/shard_map/ppermute | solution.py:419
  20.6 1.9 %collective-permute-start.2 = (bf16[1,1800,128]{2,1,0:T(8,128)(2,1)S(1)}, bf16[1,1800,128]{2,1,0:T(8,128)(2,1)S(1)}, u32[]{:S(2)}, u32[]{:S(2)}) collective-permute-start(bf16[1,1800,128]{2,1,0:T(8,128)(2,1)S(1)} %get-tuple-element.27), channel_id=1, source_target_pairs={{2,0},{4,2},{6,4},{8,6},{10,8},{12,10},{14,12},{16,14},{18,16},{20... | collective-permute-start | bytes 1382408 | tf_op jit(solution)/shard_map/ppermute | solution.py:419
  22.6 11.1 %stash.2.refs_0_ = bf16[22,1800,128]{2,1,0:T(8,128)(2,1)} custom-call(bf16[48,1800,128]{2,1,0:T(8,128)(2,1)} %x_ref.5, bf16[3,512,256]{2,1,0:T(8,128)(2,1)} %pad_maximum_fusion.1.w_ref), custom_call_target="tpu_custom_call" | custom-call | flops 5662310400 | bytes 7372800 | tf_op jit(solution)/shard_map/stash/pallas_call | solution.py:224
  33.7 0.3 collective-permute-start.3
  34.0 1.0 pad_maximum_fusion.halo_ref
  35.0 1.5 %collective-permute-done.3 = bf16[50,2,128]{2,0,1:T(8,128)(2,1)S(1)} collective-permute-done((bf16[50,2,128]{2,0,1:T(8,128)(2,1)S(1)}, bf16[50,2,128]{2,0,1:T(8,128)(2,1)S(1)}, u32[]{:S(2)}, u32[]{:S(2)}) %collective-permute-start.3) | collective-permute-done | bytes 25632 | tf_op jit(solution)/shard_map/ppermute | solution.py:419
  36.7 0.1 fusion.15
  36.8 0.1 fusion.16
  36.9 0.1 fusion.17
  37.1 0.1 fusion
  37.2 0.1 fusion.1
  37.3 0.7 pad_maximum_fusion.8.edge_ref
  38.0 1.0 copy-done.1
  39.0 5.5 %mix_modes.1.refs_0_ = bf16[48,64,128]{2,1,0:T(8,128)(2,1)} custom-call(f32[48,64,128]{2,1,0:T(8,128)} %get-tuple-element.22.own_ref, bf16[48,64,128]{2,1,0:T(8,128)(2,1)} %copy-done.1, bf16[32,2,128,128]{3,2,1,0:T(8,128)(2,1)} %refs_1_.3), custom_call_target="tpu_custom_call" | custom-call | flops 201326592 | bytes 5242880 | tf_op jit(solution)/shard_map/mix_modes/pallas_call | solution.py:134
  44.5 0.2 collective-permute-start.4
  44.7 16.7 %stash.3.stash_ref = bf16[22,1800,128]{2,1,0:T(8,128)(2,1)} custom-call(bf16[48,1800,128]{2,1,0:T(8,128)(2,1)} %x_ref.5, bf16[3,512,256]{2,1,0:T(8,128)(2,1)} %pad_maximum_fusion.1.w_ref, bf16[22,1800,128]{2,1,0:T(8,128)(2,1)} %stash.2.refs_0_), custom_call_target="tpu_custom_call", output_to_operand_aliasing={{}: (2, {})} | custom-call | flops 9909043200 | bytes 12902400 | tf_op jit(solution)/shard_map/stash/pallas_call | solution.py:224
  61.4 2.0 %collective-permute-done.4.refs_1_ = bf16[48,64,128]{2,1,0:T(8,128)(2,1)S(1)} collective-permute-done((bf16[48,64,128]{2,1,0:T(8,128)(2,1)}, bf16[48,64,128]{2,1,0:T(8,128)(2,1)S(1)}, u32[]{:S(2)}, u32[]{:S(2)}) %collective-permute-start.4) | collective-permute-done | bytes 786464 | tf_op jit(solution)/shard_map/ppermute | solution.py:419
  63.4 1.0 copy-done.2
  64.4 44.3 %block.1 = bf16[48,1800,128]{2,1,0:T(8,128)(2,1)} custom-call(s32[1]{0:T(128)} %bitcast.index_ref, bf16[48,1800,128]{2,1,0:T(8,128)(2,1)} %x_ref.5, bf16[2,1800,128]{2,1,0:T(8,128)(2,1)} %pad_maximum_fusion.halo_ref, bf16[22,1800,128]{2,1,0:T(8,128)(2,1)} %stash.3.stash_ref, bf16[3,512,256]{2,1,0:T(8,128)(2,1)} %pad_maximum_fusion.1.w_ref, ...), custom_call_target="tpu_custom_call" | custom-call | flops 28311552000 | bytes 44236800 | tf_op jit(solution)/shard_map/block/pallas_call | solution.py:380
  (18 shorter events, 0.3 us)
Async XLA Ops:
  0.0 15.5 %copy-start = (bf16[3,3,128,128]{3,2,1,0:T(8,128)(2,1)S(1)}, bf16[3,3,128,128]{3,2,1,0:T(8,128)(2,1)}, u32[]{:S(2)}) copy-start(bf16[3,3,128,128]{3,2,1,0:T(8,128)(2,1)} %param.8) | copy-start | bytes 884740
  11.3 26.7 %collective-permute-start = (bf16[48,64,128]{2,1,0:T(8,128)(2,1)}, bf16[48,64,128]{2,1,0:T(8,128)(2,1)S(1)}, u32[]{:S(2)}, u32[]{:S(2)}) collective-permute-start(bf16[48,64,128]{2,1,0:T(8,128)(2,1)} %get-tuple-element.19), channel_id=1, source_target_pairs={{0,1},{1,0},{2,3},{3,2},{4,5},{5,4},{6,7},{7,6},{8,9},{9,8},{10,11... | collective-permute-start | bytes 2359304 | tf_op jit(solution)/shard_map/ppermute | solution.py:419
  16.6 17.0 %collective-permute-start.1 = (bf16[1,1800,128]{2,1,0:T(8,128)(2,1)S(1)}, bf16[1,1800,128]{2,1,0:T(8,128)(2,1)S(1)}, u32[]{:S(2)}, u32[]{:S(2)}) collective-permute-start(bf16[1,1800,128]{2,1,0:T(8,128)(2,1)S(1)} %get-tuple-element.25), channel_id=1, source_target_pairs={{0,2},{2,4},{4,6},{6,8},{8,10},{10,12},{12,14},{14,16},{16,18},{18... | collective-permute-start | bytes 1382408 | tf_op jit(solution)/shard_map/ppermute | solution.py:419
  20.6 13.1 %collective-permute-start.2 = (bf16[1,1800,128]{2,1,0:T(8,128)(2,1)S(1)}, bf16[1,1800,128]{2,1,0:T(8,128)(2,1)S(1)}, u32[]{:S(2)}, u32[]{:S(2)}) collective-permute-start(bf16[1,1800,128]{2,1,0:T(8,128)(2,1)S(1)} %get-tuple-element.27), channel_id=1, source_target_pairs={{2,0},{4,2},{6,4},{8,6},{10,8},{12,10},{14,12},{16,14},{18,16},{20... | collective-permute-start | bytes 1382408 | tf_op jit(solution)/shard_map/ppermute | solution.py:419
  33.7 2.8 %collective-permute-start.3 = (bf16[50,2,128]{2,0,1:T(8,128)(2,1)S(1)}, bf16[50,2,128]{2,0,1:T(8,128)(2,1)S(1)}, u32[]{:S(2)}, u32[]{:S(2)}) collective-permute-start(bf16[50,2,128]{2,0,1:T(8,128)(2,1)S(1)} %pad_maximum_fusion.9), channel_id=1, source_target_pairs={{0,1},{1,0},{2,3},{3,2},{4,5},{5,4},{6,7},{7,6},{8,9},{9,8},{10,11... | collective-permute-start | bytes 76808 | tf_op jit(solution)/shard_map/ppermute | solution.py:419
  38.0 1.0 copy-start.1
  44.5 18.9 %collective-permute-start.4 = (bf16[48,64,128]{2,1,0:T(8,128)(2,1)}, bf16[48,64,128]{2,1,0:T(8,128)(2,1)S(1)}, u32[]{:S(2)}, u32[]{:S(2)}) collective-permute-start(bf16[48,64,128]{2,1,0:T(8,128)(2,1)} %mix_modes.1.refs_0_), channel_id=1, source_target_pairs={{0,1},{1,0},{2,3},{3,2},{4,5},{5,4},{6,7},{7,6},{8,9},{9,8},{10,11... | collective-permute-start | bytes 2359304 | tf_op jit(solution)/shard_map/ppermute | solution.py:419
  63.4 1.0 copy-start.2
